TPU v7x, 512 devices: a whole 4x8x8 slice. The times are simulated.
512 devices in a mesh: store: 4 (over x), seq: 16 (over y, core), tp: 8 (over z).
Axes of the slice: x: 4, y: 8, z: 8, core: 2. Of those that a mesh axis runs over, the one named last changes fastest.
Arguments:
- hidden_rows: bfloat16 [16, 128, 8192], P('seq', None, 'store'), may hold values from -6 to 6
- query_weight: bfloat16 [8192, 8, 1024], P('seq', 'tp', 'store'), may hold values from -0.0625 to 0.0625
- kv_weight: bfloat16 [8192, 2048], P('store', 'tp'), may hold values from -0.0625 to 0.0625
- cached_pages: bfloat16 [16, 64, 16, 2048], P('seq', 'store', None, 'tp'), as said below
- page_dest: int32 [16, 64], P('seq', 'store'), may hold values from -1 to 31, as said below
- rec_rows: int32 [16, 128], replicated, may hold values from 0 to 511, as said below
Outputs:
- attended: bfloat16 [16, 128, 8, 1024], P('seq', None, 'tp', 'store')
- blended: bfloat16 [16, 512, 2048], P('seq', 'store', 'tp')
Inputs may be any that keep to these rules, and one draw needn't show every extreme that they name: `page_dest`: for each passage every page number 0 to 31 stands in exactly one slot and the other slots hold -1. Slots of one store index hold at most 4 page numbers of one aligned run of 8, and in every passage some store index holds exactly 4 of each run. `rec_rows`: each passage lists 128 distinct rows in rising order, always its first and its last row. `cached_pages`: pages in slots that hold -1 are never read.
All inputs are finite; a program needn't handle non-finite values.
Results may differ from a plain program's by a relative error of at most 0.023.
Values may be sent and summed in bfloat16 or wider, within the bound.
A program may use at most 64 MiB of HBM per device.

v0:
```python
import jax
import jax.numpy as jnp
from jax import lax
from jax.sharding import PartitionSpec as P

HD = 128
PASSAGE = 512


rope_base = 500000.0
masked_score = -1e30


def rotate(values, places):
    half_width = values.shape[-1] // 2
    frequency = rope_base ** (-(jnp.arange(half_width, dtype=jnp.float32) * 2.0 / values.shape[-1]))
    angles = places.astype(jnp.float32)[:, None] * frequency[None, :]
    cosine = jnp.cos(angles)[:, None, :]
    sine_part = jnp.sin(angles)[:, None, :]
    first_half = values[..., :half_width]
    second = values[..., half_width:]
    return jnp.concatenate(
        [first_half * cosine - second * sine_part, second * cosine + first_half * sine_part],
        axis=-1,
    )


def keep_state(state_now):
    return state_now


def absorb(state_now, group_queries, group_places, key_rows, value_rows, key_places):

    def update(old_state):
        old_max, old_sum, old_accumulated = old_state
        scores = jnp.einsum(
            "rkqd,tkd->kqrt", group_queries, key_rows, preferred_element_type=jnp.float32
        )
        visible = key_places[None, None, None, :] <= group_places[None, None, :, None]
        scores = jnp.where(visible, scores, masked_score)
        new_max = jnp.maximum(old_max, jnp.max(scores, axis=-1))
        weights = jnp.exp(scores - new_max[..., None])
        new_sum = jnp.sum(weights, axis=-1)
        product = jnp.einsum(
            "kqrt,tkd->kqrd",
            weights.astype(jnp.bfloat16),
            value_rows,
            preferred_element_type=jnp.float32,
        )
        return (new_max, new_sum, product)

    return lax.cond(jnp.min(key_places) <= jnp.max(group_places), update, keep_state, state_now)


def on_device(hidden_rows, query_weight, kv_weight, cached_pages, page_dest, rec_rows):
    store_count = lax.axis_size("store")
    seq_count = lax.axis_size("seq")
    store_index = lax.axis_index("store")
    seq_index = lax.axis_index("seq")
    local_rows = hidden_rows[0]
    rec_count = local_rows.shape[0]
    chosen = lax.dynamic_index_in_dim(rec_rows, seq_index, 0, keepdims=False)
    places = seq_index * PASSAGE + chosen
    kv_heads = query_weight.shape[1]
    local_group = query_weight.shape[2] // HD
    kv_width = kv_weight.shape[1]
    full_rows = lax.all_gather(local_rows, "store", axis=1, tiled=True)

    def add_rows(shard_piece):
        flat_piece = shard_piece.reshape(shard_piece.shape[0], -1)
        return jnp.dot(full_rows, flat_piece, preferred_element_type=jnp.float32)

    query_sums = add_rows(lax.all_gather(query_weight, "seq", axis=0, tiled=True))
    queries = rotate(query_sums.reshape(rec_count, kv_heads * local_group, HD), places) * HD ** (
        -0.5
    )
    queries = queries.astype(jnp.bfloat16).reshape(rec_count, kv_heads, local_group, HD)
    fresh_rows = add_rows(lax.all_gather(kv_weight, "store", axis=0, tiled=True))
    fresh_rows = fresh_rows.reshape(rec_count, kv_heads, 2 * HD)
    fresh_kv = jnp.concatenate(
        [rotate(fresh_rows[..., :HD], places), fresh_rows[..., HD:]], axis=-1
    )
    fresh_kv = fresh_kv.astype(jnp.bfloat16).reshape(rec_count, kv_width)
    page_block = cached_pages[0]
    targets = page_dest[0]
    pool_size = page_block.shape[0]
    page_rows = page_block.shape[1]
    row_count = PASSAGE // store_count
    page_count = row_count // page_rows
    capacity = page_count // 2
    pool_order = jnp.arange(pool_size)
    owners = jnp.where(targets >= 0, targets // page_count, -1)
    earlier = (owners[None, :] == owners[:, None]) & (pool_order[None, :] < pool_order[:, None])
    rank_index = jnp.sum(earlier.astype(jnp.int32), axis=1)
    slot_index = jnp.where(targets >= 0, owners * capacity + rank_index, -1)
    send_slots = jnp.arange(store_count * capacity)
    placing = slot_index[None, :] == send_slots[:, None]
    outgoing = jnp.dot(
        placing.astype(jnp.bfloat16),
        page_block.reshape(pool_size, -1),
        preferred_element_type=jnp.float32,
    )
    outgoing = outgoing.astype(jnp.bfloat16).reshape(store_count, capacity, page_rows, kv_width)
    page_ids = jnp.sum(jnp.where(placing, targets[None, :] % page_count + 1, 0), axis=1) - 1
    page_ids = page_ids.reshape(store_count, capacity)
    arrived, arrived_ids = (
        lax.all_to_all(outgoing, "store", split_axis=0, concat_axis=0, tiled=True),
        lax.all_to_all(page_ids, "store", split_axis=0, concat_axis=0, tiled=True),
    )
    ordering = arrived_ids.reshape(-1)[None, :] == jnp.arange(page_count)[:, None]
    reused = jnp.dot(
        ordering.astype(jnp.bfloat16),
        arrived.reshape(store_count * capacity, -1),
        preferred_element_type=jnp.float32,
    )
    reused = reused.astype(jnp.bfloat16).reshape(row_count, kv_width)
    own_rows = store_index * row_count + jnp.arange(row_count)
    matches = own_rows[:, None] == chosen[None, :]
    replaced = jnp.dot(
        matches.astype(jnp.bfloat16), fresh_kv, preferred_element_type=jnp.float32
    ).astype(jnp.bfloat16)
    blended = jnp.where(jnp.any(matches, axis=1)[:, None], replaced, reused)
    groups = [(queries, places)]
    initial = tuple(
        (
            (
                jnp.full(
                    (kv_heads, local_group, query_group[0].shape[0]), masked_score, jnp.float32
                ),
                jnp.zeros((kv_heads, local_group, query_group[0].shape[0]), jnp.float32),
                jnp.zeros((kv_heads, local_group, query_group[0].shape[0], HD), jnp.float32),
            )
            for query_group in groups
        )
    )

    def consume(carried, flat_keys, key_places):
        head_rows = flat_keys.reshape(flat_keys.shape[0], kv_heads, 2 * HD)
        key_rows = head_rows[..., :HD]
        value_rows = head_rows[..., HD:]
        return tuple(
            (
                absorb(state_now, query_group[0], query_group[1], key_rows, value_rows, key_places)
                for state_now, query_group in zip(carried, groups)
            )
        )

    shard_piece = lax.all_gather(blended[None], ("store", "seq"), axis=0, tiled=True)
    shard_ids = jnp.arange(shard_piece.shape[0])
    base_rows = shard_ids % seq_count * PASSAGE + shard_ids // seq_count * row_count
    key_places = (base_rows[:, None] + jnp.arange(shard_piece.shape[1])[None, :]).reshape(-1)
    results = consume(initial, shard_piece.reshape(-1, kv_width), key_places)

    def finish(state_now):
        accumulated = state_now[2] / state_now[1][..., None]
        ordered = jnp.transpose(accumulated, (2, 0, 1, 3))
        return ordered.reshape(ordered.shape[0], kv_heads, local_group * HD).astype(jnp.bfloat16)

    finished = [finish(state_now) for state_now in results]
    attended = finished[0]
    return (attended[None], blended[None])


def solution(mesh):
    placed = (
        P("seq", None, "store"),
        P("seq", "tp", "store"),
        P("store", "tp"),
        P("seq", "store", None, "tp"),
        P("seq", "store"),
        P(),
    )
    return jax.shard_map(
        on_device,
        mesh=mesh,
        in_specs=placed,
        out_specs=(P("seq", None, "tp", "store"), P("seq", "store", "tp")),
        check_vma=False,
    )
```

profile of v0, /device:TPU:1, one launch (start us, length us, event | category | flops | bytes accessed | tf_op | source)
XLA Modules:
  0.0 259.8 jit_solution(8228149113488179572)
XLA Ops:
  7.2 0.0 all-gather.11.cloned.1.call-start
  7.2 0.7 all-gather.11.cloned.1.call-update
  7.9 0.0 all-gather.7.cloned.1.call-start
  7.9 0.7 all-gather.7.cloned.1.call-update
  8.6 0.0 all-gather.9.cloned.1.call-start
  8.7 0.7 all-gather.9.cloned.1.call-update
  9.4 0.7 fusion.57
  10.0 0.7 compare_select_fusion
  10.7 0.2 convert_reduce_fusion
  10.9 0.7 fusion.49
  11.6 0.1 select_reduce_fusion
  11.7 0.7 sub.40
  12.4 4.8 %all-to-all-start = ((s32[4,1,4]{2,1,0:T(1,128)}), s32[4,1,4]{2,1,0:T(1,128)S(1)}, u32[]{:S(2)}, u32[]{:S(2)}) async-start(s32[4,1,4]{2,1,0:T(1,128)} %bitcast.23), calls=%async_computation | async-start | bytes 4096 | tf_op jit(solution)/shard_map/all_to_all | solution.py:108
  17.2 0.9 copy.23
  18.1 0.2 convolution_convert_fusion
  18.3 0.7 copy.24
  19.0 0.7 fusion.51
  19.7 0.2 compare_reduce_fusion
  19.9 1.4 all-to-all-done
  21.2 3.3 %all-to-all-start.1 = ((bf16[4,4,16,256]{3,2,1,0:T(8,128)(2,1)}), bf16[4,4,16,256]{3,2,1,0:T(8,128)(2,1)S(1)}, u32[]{:S(2)}, u32[]{:S(2)}) async-start(bf16[4,4,16,256]{3,2,1,0:T(8,128)(2,1)} %bitcast.42), calls=%async_computation.1 | async-start | bytes 262144 | tf_op jit(solution)/shard_map/all_to_all | solution.py:107
  24.6 0.0 all-gather.13.cloned.1.call-start
  24.6 0.5 broadcast.316
  25.1 0.7 reduce.8
  25.8 0.1 eq.70
  25.9 3.5 %all-to-all-done.1 = bf16[4,4,16,256]{3,2,1,0:T(8,128)(2,1)S(1)} async-done(((bf16[4,4,16,256]{3,2,1,0:T(8,128)(2,1)}), bf16[4,4,16,256]{3,2,1,0:T(8,128)(2,1)S(1)}, u32[]{:S(2)}, u32[]{:S(2)}) %all-to-all-start.1) | async-done | bytes 131104 | tf_op jit(solution)/shard_map/all_to_all | solution.py:107
  29.4 0.1 convolution_convert_fusion.1
  29.6 22.9 %all-gather.11.cloned.1.call-done = bf16[1,128,8192]{2,1,0:T(8,128)(2,1)} async-done(((bf16[1,128,2048]{2,1,0:T(8,128)(2,1)}), bf16[1,128,8192]{2,1,0:T(8,128)(2,1)}) %all-gather.11.cloned.1.call-update) | async-done | bytes 2097168 | tf_op jit(solution)/shard_map/all_gather | solution.py:67
  52.5 55.1 %all-gather.7.cloned.1.call-done = bf16[8192,256]{1,0:T(8,128)(2,1)} async-done(((bf16[2048,256]{1,0:T(8,128)(2,1)}), bf16[8192,256]{1,0:T(8,128)(2,1)}) %all-gather.7.cloned.1.call-update) | async-done | bytes 4194320 | tf_op jit(solution)/shard_map/all_gather | solution.py:78
  107.7 3.5 %fusion.15 = f32[128,1,256]{2,0,1:T(8,128)S(1)} fusion(bf16[8192,256]{1,0:T(8,128)(2,1)} %all-gather.7.cloned.1.call-done, bf16[1,128,8192]{2,1,0:T(8,128)(2,1)} %all-gather.11.cloned.1.call-done), kind=kOutput, calls=%fused_computation.20 | convolution fusion | flops 536870912 | bytes 6422528 | tf_op jit(solution)/shard_map/dot_general | solution.py:71
  111.2 0.3 fusion.39
  111.5 0.9 fusion.18
  112.4 0.0 all-gather.13.cloned.1.call-update
  112.4 0.6 reduce_max.18
  113.0 0.7 iota_add_fusion
  114.9 0.2 multiply_cosine_fusion.1
  115.1 40.0 %all-gather.9.cloned.1.call-done = bf16[8192,1,256]{2,0,1:T(8,128)(2,1)} async-done(((bf16[512,1,256]{2,0,1:T(8,128)(2,1)}), bf16[8192,1,256]{2,0,1:T(8,128)(2,1)}) %all-gather.9.cloned.1.call-update) | async-done | bytes 4194320 | tf_op jit(solution)/shard_map/all_gather | solution.py:73
  155.2 0.0 copy-start
  155.2 6.5 %copy.19 = bf16[256,8192]{1,0:T(8,128)(2,1)} copy(bf16[256,8192]{0,1:T(8,128)(2,1)} %bitcast.101) | data formatting | bytes 8388608 | tf_op jit(solution)/shard_map/dot_general | solution.py:71
  161.7 0.0 copy-done
  161.7 3.4 %fusion.11 = f32[128,2,128]{0,2,1:T(8,128)S(1)} fusion(bf16[2,128,8192]{2,1,0:T(8,128)(2,1)} %bitcast.100, bf16[1,128,8192]{2,1,0:T(8,128)(2,1)S(1)} %copy-done), kind=kOutput, calls=%fused_computation.16 | convolution fusion | flops 536870912 | bytes 6422528 | tf_op jit(solution)/shard_map/dot_general | solution.py:71
  165.2 77.4 %all-gather.13.cloned.1.call-done = bf16[8192,256]{1,0:T(8,128)(2,1)} async-done(((bf16[128,256]{1,0:T(8,128)(2,1)}), bf16[8192,256]{1,0:T(8,128)(2,1)}) %all-gather.13.cloned.1.call-update) | async-done | bytes 4194320 | tf_op jit(solution)/shard_map/all_gather | solution.py:148
  242.6 9.8 %conditional.1 = (f32[1,2,128]{2,1,0:T(2,128)S(1)}, f32[1,2,128,128]{3,2,1,0:T(8,128)S(1)}) conditional(s32[]{:T(128)} %convert_element_type.62, () %tuple.19, (s32[64,128]{1,0:T(8,128)S(1)}, s32[128]{0:T(128)S(1)}, bf16[64,128,256]{2,1,0:T(8,128)(2,1)}, bf16[128,1,2,128]{0,3,2,1:T(8,128)(2,1)S(1)}) %tuple.44), branch_computations={%region_5.6_spmd, %region_6.9_spmd} | conditional | flops 1087373056 | bytes 48470572 | solution.py:52
  242.6 3.7 %broadcast_compare_fusion = pred[128,8192]{0,1:T(8,128)(4,1)S(1)} fusion(s32[128]{0:T(128)S(1)} %get-tuple-element.21, s32[8192]{0:T(1024)S(1)} %bitcast.109), kind=kLoop, calls=%fused_computation.10 | loop fusion | flops 1048576 | bytes 1081856 | tf_op jit(solution)/shard_map/cond/branch_1_fun/le | solution.py:39
  246.3 0.0 copy-start.1
  246.3 3.3 %fusion.52 = (f32[2,128]{1,0:T(2,128)S(1)}, f32[1,2,128,8192]{2,3,1,0:T(8,128)S(1)}) fusion(bf16[128,1,2,128]{0,3,2,1:T(8,128)(2,1)S(1)} %get-tuple-element.41, bf16[8192,1,256]{2,0,1:T(8,128)(2,1)} %bitcast.103, pred[128,8192]{0,1:T(8,128)(4,1)S(1)} %broadcast_compare_fusion), kind=kOutput, calls=%fused_computation.96 | convolution fusion | flops 541064960 | bytes 11600896 | tf_op jit(solution)/shard_map/cond/branch_1_fun/rkqd,tkd->kqrt/dot_general | solution.py:36
  249.6 0.0 copy-done.1
  249.6 1.7 fusion.7
  251.3 1.1 fusion.2
  252.4 0.1 fusion.34
  252.5 0.1 copy.21
  252.6 0.7 convert_element_type.71
  (9 shorter events, 0.2 us)
Async XLA Ops:
  7.2 45.4 %all-gather.11.cloned.1.call-start = ((), (), s32[]{:S(2)}) async-start(), calls=%async_computation.4 | async-start | bytes 2621440 | tf_op jit(solution)/shard_map/all_gather | solution.py:67
  7.9 99.8 %all-gather.7.cloned.1.call-start = ((), (), s32[]{:S(2)}) async-start(), calls=%async_computation.2 | async-start | bytes 5242880 | tf_op jit(solution)/shard_map/all_gather | solution.py:78
  8.6 146.5 %all-gather.9.cloned.1.call-start = ((), (), s32[]{:S(2)}) async-start(), calls=%async_computation.3 | async-start | bytes 4456448 | tf_op jit(solution)/shard_map/all_gather | solution.py:73
  12.4 8.9 %all-to-all-start = ((s32[4,1,4]{2,1,0:T(1,128)}), s32[4,1,4]{2,1,0:T(1,128)S(1)}, u32[]{:S(2)}, u32[]{:S(2)}) async-start(s32[4,1,4]{2,1,0:T(1,128)} %bitcast.23), calls=%async_computation | async-start | bytes 4096 | tf_op jit(solution)/shard_map/all_to_all | solution.py:108
  21.2 8.1 %all-to-all-start.1 = ((bf16[4,4,16,256]{3,2,1,0:T(8,128)(2,1)}), bf16[4,4,16,256]{3,2,1,0:T(8,128)(2,1)S(1)}, u32[]{:S(2)}, u32[]{:S(2)}) async-start(bf16[4,4,16,256]{3,2,1,0:T(8,128)(2,1)} %bitcast.42), calls=%async_computation.1 | async-start | bytes 262144 | tf_op jit(solution)/shard_map/all_to_all | solution.py:107
  24.6 218.0 %all-gather.13.cloned.1.call-start = ((), (), s32[]{:S(2)}) async-start(), calls=%async_computation.5 | async-start | bytes 4259840 | tf_op jit(solution)/shard_map/all_gather | solution.py:148
  155.2 6.5 %copy-start = (bf16[1,128,8192]{2,1,0:T(8,128)(2,1)S(1)}, bf16[1,128,8192]{2,1,0:T(8,128)(2,1)}, u32[]{:S(2)}) copy-start(bf16[1,128,8192]{2,1,0:T(8,128)(2,1)} %all-gather.11.cloned.1.call-done) | copy-start | bytes 6291460
  246.3 3.3 %copy-start.1 = (bf16[64,128,256]{2,1,0:T(8,128)(2,1)S(1)}, bf16[64,128,256]{2,1,0:T(8,128)(2,1)}, u32[]{:S(2)}) copy-start(bf16[64,128,256]{2,1,0:T(8,128)(2,1)} %get-tuple-element.22) | copy-start | bytes 12582916 | tf_op jit(solution)/shard_map/cond
Sparse Core Ops, SparseCore 0:
  10.1 42.3 all-gather.10
  54.6 52.9 all-gather.6
  109.8 45.3 all-gather.8
  159.0 83.5 all-gather.12
where the time goes:
time: 260 us
  waiting for transfers between devices  202 us (78%)
  between operations  15.1 us (6%)
  matrix products  13.1 us (5%)
  other arithmetic  10.6 us (4%)
  local copies, waits for them, and re-layouts  10.2 us (4%)
  starting transfers between devices  8.32 us (3%)
    all_gather x1, waiting for transfers between devices, on_device(): lax.all_gather(blended[None], ('store', 'seq'), axis=0, tiled=True)  77.4 us
    all_gather x1, waiting for transfers between devices, on_device(): lax.all_gather(kv_weight, 'store', axis=0, tiled=True)  55.1 us
    all_gather x1, waiting for transfers between devices, on_device(): lax.all_gather(query_weight, 'seq', axis=0, tiled=True)  40 us
    all_gather x1, waiting for transfers between devices, on_device(): full_rows = lax.all_gather(local_rows, 'store', axis=1, tiled=True)  22.9 us
    dot_general x2, matrix products, add_rows(): return jnp.dot(full_rows, flat_piece, preferred_element_type=jnp.float32)  6.96 us
    dot_general x1, local copies, waits for them, and re-layouts, add_rows(): return jnp.dot(full_rows, flat_piece, preferred_element_type=jnp.float32)  6.5 us
  transfers between devices with their start and end apart: 6, of which 6 were waited for; matrix products, arithmetic and copies ran while one was open for 9% of the time, Pallas kernels for 0%

commit v1 on v0

v1 whole, which is shorter than its diff:
```python
import functools

import jax
import jax.numpy as jnp
import numpy as np
from jax import lax
from jax.experimental import pallas as pl
from jax.experimental.pallas import tpu as pltpu
from jax.sharding import PartitionSpec as P

HD = 128
PASSAGE = 512
PAGE = 16
REC = 128
ROWS = 128
NX, NY = 4, 8
DEPTH = 1024
SLOTS = 16
ROPE_BASE = 500000.0
MASKED = -1e30
QUERY_SCALE = HD**-0.5 * 1.4426950408889634
F32 = jnp.float32
BF16 = jnp.bfloat16
LOGICAL = pl.DeviceIdType.MESH


def wrap(value, count):
    return lax.rem(value, count)


def rotate(values, cosine, signed_sine):
    return values * cosine + pltpu.roll(values, HD // 2, 1) * signed_sine


def kernel(
    hid_hbm, wq_hbm, kvw_hbm, pages_hbm, dest_hbm, rec_hbm, freq_hbm,
    att_hbm, blend_hbm,
    dest_smem, rec_ref, freq_ref, kvw, pages, hall, wall, cont, cont_in, kv_all, v_t,
    q_all, scores, o_out, s_out, o_in, s_in, att,
    local_sem, h_send, h_recv, w_send, w_recv, ws_send, ws_recv,
    c_send, c_recv, kv_send, kv_recv, ks_send, ks_recv,
    q_send, q_recv, o_send, o_recv, s_send, s_recv,
):
    x = lax.axis_index("store")
    sq = lax.axis_index("seq")
    z = lax.axis_index("tp")
    y = sq // 2
    c = wrap(sq, 2)

    def dev(x_to=None, y_to=None, c_to=None, z_to=None):
        x_at = x if x_to is None else x_to
        y_at = y if y_to is None else y_to
        c_at = c if c_to is None else c_to
        z_at = z if z_to is None else z_to
        return (x_at, y_at * 2 + c_at, z_at)

    def remote(src, dst, send_sem, recv_sem, target):
        return pltpu.make_async_remote_copy(
            src_ref=src, dst_ref=dst, send_sem=send_sem, recv_sem=recv_sem,
            device_id=target, device_id_type=LOGICAL,
        )

    def arrived(ref, sem):
        pltpu.make_async_copy(ref, ref, sem).wait()

    sent = []

    def start(copy):
        copy.start()
        sent.append(copy)

    def sent_all():
        for copy in sent:
            copy.wait_send()

    load_hid = pltpu.make_async_copy(hid_hbm, hall.at[x], local_sem.at[0])
    load_kvw = pltpu.make_async_copy(kvw_hbm, kvw, local_sem.at[1])
    load_pages = pltpu.make_async_copy(pages_hbm, pages, local_sem.at[2])
    load_wq = pltpu.make_async_copy(wq_hbm, wall.at[y, c], local_sem.at[3])
    load_dest = pltpu.make_async_copy(dest_hbm, dest_smem, local_sem.at[4])
    load_rec = pltpu.make_async_copy(rec_hbm, rec_ref, local_sem.at[5])
    load_freq = pltpu.make_async_copy(freq_hbm, freq_ref, local_sem.at[6])
    load_rec.start()
    load_freq.start()
    load_hid.start()
    load_kvw.start()
    load_dest.start()
    load_pages.start()
    load_wq.start()

    barrier = pltpu.get_barrier_semaphore()

    def greet(target):
        pl.semaphore_signal(barrier, inc=1, device_id=target, device_id_type=LOGICAL)

    for off in range(1, NX):
        greet(dev(x_to=wrap(x + off, NX)))
    for off in (1, NY - 1):
        greet(dev(y_to=wrap(y + off, NY)))
    greet(dev(c_to=1 - c))

    load_rec.wait()
    load_freq.wait()
    chosen = rec_ref[pl.ds(sq, 1), :]
    row_iota = lax.broadcasted_iota(jnp.int32, (REC, REC), 0)
    lane_iota = lax.broadcasted_iota(jnp.int32, (REC, REC), 1)
    chosen_wide = jnp.broadcast_to(chosen, (REC, REC))
    chosen_col = jnp.sum(
        jnp.where(row_iota == lane_iota, chosen_wide.astype(F32), 0.0), axis=1, keepdims=True
    )
    places = chosen_col + (sq * PASSAGE).astype(F32)
    angles = places * freq_ref[...]
    cosine = jnp.cos(angles)
    sine = jnp.sin(angles)
    signed_sine = jnp.where(lane_iota < HD // 2, -sine, sine)

    load_hid.wait()
    load_kvw.wait()
    fresh = jnp.dot(hall[x], kvw[...], preferred_element_type=F32)
    fresh_keys = rotate(fresh[:, :HD], cosine, signed_sine).astype(BF16)
    fresh_values = fresh[:, HD:].astype(BF16)
    fresh_bf = jnp.concatenate([fresh_keys, fresh_values], axis=1)

    lane_wide = lax.broadcasted_iota(jnp.int32, (1, SLOTS * PAGE), 1)
    target = jnp.full((1, SLOTS * PAGE), -1, jnp.int32)
    load_dest.wait()
    for slot in range(SLOTS):
        page_at = dest_smem[0, slot]
        base = jnp.where(page_at >= 0, page_at * PAGE, -PASSAGE)
        target = jnp.where(lane_wide // PAGE == slot, base + wrap(lane_wide, PAGE), target)
    load_pages.wait()
    for part in range(NX):
        part_rows = lax.broadcasted_iota(jnp.int32, (ROWS, REC), 0) + part * ROWS
        hit = part_rows == chosen_wide
        pick_fresh = jnp.where(hit, 1.0, 0.0)
        keep = 1.0 - jnp.max(pick_fresh, axis=1, keepdims=True)
        wide_rows = lax.broadcasted_iota(jnp.int32, (ROWS, SLOTS * PAGE), 0) + part * ROWS
        pick_page = jnp.where(wide_rows == target, 1.0, 0.0) * keep
        term = jnp.dot(pick_fresh.astype(BF16), fresh_bf, preferred_element_type=F32)
        term = term + jnp.dot(pick_page.astype(BF16), pages[...], preferred_element_type=F32)
        cont[part] = term.astype(BF16)

    pl.semaphore_wait(barrier, 6)

    for off in range(1, NX):
        x_to = wrap(x + off, NX)
        start(
            remote(
                cont.at[x_to], cont_in.at[off - 1], c_send.at[off - 1], c_recv.at[off - 1],
                dev(x_to=x_to),
            )
        )

    right, left, far = wrap(x + 1, NX), wrap(x + NX - 1, NX), wrap(x + 2, NX)
    other = 1 - c
    up, down = dev(y_to=wrap(y + 1, NY)), dev(y_to=wrap(y + NY - 1, NY))

    def half(at):
        return pl.ds(at * DEPTH // 4, DEPTH // 4)

    def weight_below(step):
        return wall.at[wrap(y + NY - step, NY), c]

    def weight_above(step):
        return wall.at[wrap(y + step, NY), c]

    def weight_up(src, block, step, at):
        start(
            remote(
                src.at[half(at)], block.at[half(at)], w_send.at[0, step, at],
                w_recv.at[0, step, at], up,
            )
        )

    def weight_down(src, block, step, at):
        start(
            remote(
                src.at[half(at)], block.at[half(at)], w_send.at[1, step, at],
                w_recv.at[1, step, at], down,
            )
        )

    def weight_core(src, block, step):
        start(remote(src, block, ws_send.at[step], ws_recv.at[step], dev(c_to=other)))

    own = wall.at[y, c]
    weight_up(wq_hbm, own, 0, 0)
    weight_down(wq_hbm, own, 0, 1)
    weight_up(wq_hbm, own, 0, 1)
    weight_down(wq_hbm, own, 0, 0)
    weight_core(wq_hbm, own, 0)

    def weight_relay(step):
        for at in range(2):
            arrived(weight_below(step).at[half(at)], w_recv.at[0, step - 1, at])
            if step < 3 or at == 0:
                weight_up(weight_below(step), weight_below(step), step, at)
            arrived(weight_above(step).at[half(1 - at)], w_recv.at[1, step - 1, 1 - at])
            if step < 3 or at == 0:
                weight_down(weight_above(step), weight_above(step), step, 1 - at)
        weight_core(weight_below(step), weight_below(step), 2 * step - 1)
        weight_core(weight_above(step), weight_above(step), 2 * step)

    def piece(at):
        return pl.ds(at * DEPTH // 2, DEPTH // 2)

    def hidden_right(src, block, step, at):
        start(
            remote(
                src.at[:, piece(at)], block.at[:, piece(at)], h_send.at[0, step],
                h_recv.at[0, step], dev(x_to=right),
            )
        )

    def hidden_left(src, block, step, at):
        start(
            remote(
                src.at[:, piece(at)], block.at[:, piece(at)], h_send.at[1, step],
                h_recv.at[1, step], dev(x_to=left),
            )
        )

    for at in range(4):
        hidden_right(hid_hbm, hall.at[x], at, at)
        hidden_left(hid_hbm, hall.at[x], 3 - at, 3 - at)

    total = cont[x].astype(F32)
    for off in range(1, NX):
        arrived(cont_in.at[off - 1], c_recv.at[off - 1])
        total = total + cont_in[off - 1].astype(F32)
    kv_all[sq] = total.astype(BF16)
    save_blend = pltpu.make_async_copy(kv_all.at[sq], blend_hbm, local_sem.at[0])
    save_blend.start()

    low_rows, high_rows = pl.ds(0, ROWS // 2), pl.ds(ROWS // 2, ROWS // 2)

    def pass_up(block, step):
        start(remote(block, block, kv_send.at[step], kv_recv.at[step], up))

    def pass_down(block, step):
        start(remote(block, block, kv_send.at[4 + step], kv_recv.at[4 + step], down))

    def pass_core(block, step):
        start(remote(block, block, ks_send.at[step], ks_recv.at[step], dev(c_to=other)))

    def below(step):
        return kv_all.at[wrap(y + NY - step, NY) * 2 + c]

    def above(step):
        return kv_all.at[wrap(y + step, NY) * 2 + c]

    def relay(step):
        arrived(below(step), kv_recv.at[step - 1])
        if step < 3:
            pass_up(below(step), step)
        else:
            pass_up(below(step).at[low_rows], step)
        arrived(above(step), kv_recv.at[4 + step - 1])
        if step < 3:
            pass_down(above(step), step)
        else:
            pass_down(above(step).at[high_rows], step)
        pass_core(below(step), 2 * step - 1)
        pass_core(above(step), 2 * step)

    pass_up(kv_all.at[sq], 0)
    pass_down(kv_all.at[sq], 0)
    pass_core(kv_all.at[sq], 0)

    weight_relay(1)
    for at in range(2):
        arrived(hall.at[left, :, piece(at)], h_recv.at[0, at])
        hidden_right(hall.at[left], hall.at[left], 4 + at, at)
        arrived(hall.at[right, :, piece(3 - at)], h_recv.at[1, 3 - at])
        hidden_left(hall.at[right], hall.at[right], 5 - at, 3 - at)

    weight_relay(2)
    relay(1)
    weight_relay(3)
    relay(2)
    relay(3)

    for at in range(2):
        arrived(hall.at[left, :, piece(2 + at)], h_recv.at[0, 2 + at])
        arrived(hall.at[right, :, piece(at)], h_recv.at[1, at])
    for at in range(2):
        arrived(hall.at[far, :, piece(at)], h_recv.at[0, 4 + at])
        arrived(hall.at[far, :, piece(2 + at)], h_recv.at[1, 4 + at])
    load_wq.wait()

    def term(chip):
        lanes = pl.ds(pl.multiple_of(wrap(chip, 2) * DEPTH, DEPTH), DEPTH)
        return jnp.dot(
            hall[chip // 2, :, lanes], wall[chip].reshape(DEPTH, 2 * HD),
            preferred_element_type=F32,
        )

    arrived(wall.at[y, other], ws_recv.at[0])
    q_sum = term(y)
    for step in range(1, 4):
        below_at, above_at = wrap(y + NY - step, NY), wrap(y + step, NY)
        arrived(wall.at[below_at, other], ws_recv.at[2 * step - 1])
        q_sum = q_sum + term(below_at)
        arrived(wall.at[above_at, other], ws_recv.at[2 * step])
        q_sum = q_sum + term(above_at)
    opposite = wrap(y + 4, NY)
    arrived(weight_below(4).at[half(0)], w_recv.at[0, 3, 0])
    arrived(weight_below(4).at[half(1)], w_recv.at[1, 3, 1])
    weight_core(weight_below(4), weight_below(4), 7)
    arrived(wall.at[opposite, other], ws_recv.at[7])
    q_sum = q_sum + term(opposite)

    for head in range(2):
        turned = rotate(q_sum[:, head * HD : (head + 1) * HD], cosine, signed_sine)
        q_all[x, pl.ds(head * REC, REC), :] = (turned * QUERY_SCALE).astype(BF16)
    for off in (2, 1, 3):
        start(
            remote(
                q_all.at[x], q_all.at[x], q_send.at[off], q_recv.at[off],
                dev(x_to=wrap(x + off, NX)),
            )
        )

    arrived(below(4).at[low_rows], kv_recv.at[3])
    arrived(below(4).at[high_rows], kv_recv.at[7])
    pass_core(below(4), 7)
    arrived(kv_all.at[2 * y + other], ks_recv.at[0])
    for step in range(1, 4):
        arrived(kv_all.at[wrap(y + NY - step, NY) * 2 + other], ks_recv.at[2 * step - 1])
        arrived(kv_all.at[wrap(y + step, NY) * 2 + other], ks_recv.at[2 * step])
    arrived(kv_all.at[wrap(y + 4, NY) * 2 + other], ks_recv.at[7])

    def turn(at, carry):
        lanes = pl.ds(pl.multiple_of(at * ROWS, ROWS), ROWS)
        v_t[:, lanes] = kv_all[at, :, HD:].astype(F32).T.astype(BF16)
        return carry

    lax.fori_loop(0, 2 * NY, turn, 0)

    pair = 2 * ROWS
    key_row = lax.broadcasted_iota(jnp.int32, (pair, 2 * REC), 0)
    key_place = (
        (2 * y + key_row // ROWS) * PASSAGE + x * ROWS + wrap(key_row, ROWS)
    )
    query_place = jnp.concatenate([chosen, chosen], axis=1) + sq * PASSAGE

    def attend(off):
        to = wrap(x + off, NX)
        if off:
            arrived(q_all.at[to], q_recv.at[NX - off])
        query = q_all[to]

        def score(at):
            keys = kv_all[pl.ds(2 * at, 2), :, :HD].reshape(pair, HD)
            return lax.dot_general(
                keys, query, (((1,), (1,)), ((), ())), preferred_element_type=F32
            )

        def first(at, top):
            value = score(at)
            scores[at] = value
            return jnp.maximum(top, jnp.max(value.reshape(pair // 8, 8, 2 * REC), axis=0))

        top = lax.fori_loop(0, y, first, jnp.full((8, 2 * REC), MASKED, F32))
        value = jnp.where(key_place <= query_place, score(y), MASKED)
        scores[y] = value
        top = jnp.maximum(top, jnp.max(value.reshape(pair // 8, 8, 2 * REC), axis=0))
        top = jnp.max(top, axis=0, keepdims=True)

        def second(at, carry):
            sums, mixture = carry
            weights = jnp.exp2(scores[at] - top)
            sums = sums + jnp.sum(weights.reshape(pair // 8, 8, 2 * REC), axis=0)
            values = v_t[:, pl.ds(pl.multiple_of(at * pair, pair), pair)]
            mixture = mixture + jnp.dot(
                values, weights.astype(BF16), preferred_element_type=F32
            )
            return sums, mixture

        sums, mixture = lax.fori_loop(
            0, y + 1, second,
            (jnp.zeros((8, 2 * REC), F32), jnp.zeros((HD, 2 * REC), F32)),
        )
        sums = jnp.sum(sums, axis=0, keepdims=True)
        o_out[off] = mixture.astype(BF16)
        s_out[off, 0:1, :] = top
        s_out[off, 1:2, :] = sums
        s_out[off, 2:8, :] = jnp.zeros((6, 2 * REC), F32)
        if off:
            start(
                remote(o_out.at[off], o_in.at[off], o_send.at[off], o_recv.at[off], dev(x_to=to))
            )
            start(
                remote(s_out.at[off], s_in.at[off], s_send.at[off], s_recv.at[off], dev(x_to=to))
            )

    attend(0)
    attend(1)
    attend(3)
    attend(2)

    for off in (1, 3, 2):
        arrived(o_in.at[off], o_recv.at[off])
        arrived(s_in.at[off], s_recv.at[off])
    s_in[0] = s_out[0]
    o_in[0] = o_out[0]
    tops = [s_in[off, 0:1, :] for off in range(NX)]
    parts = [s_in[off, 1:2, :] for off in range(NX)]
    top = jnp.maximum(jnp.maximum(tops[0], tops[1]), jnp.maximum(tops[2], tops[3]))
    factors = [jnp.exp2(value - top) for value in tops]
    whole = sum(part * factor for part, factor in zip(parts, factors))
    mixed = sum(o_in[off].astype(F32) * factors[off] for off in range(NX))
    mixed = mixed / whole
    for head in range(2):
        att[:, head * HD : (head + 1) * HD] = (
            mixed[:, head * REC : (head + 1) * REC].T.astype(BF16)
        )
    save_att = pltpu.make_async_copy(att, att_hbm, local_sem.at[1])
    save_att.start()

    sent_all()
    save_blend.wait()
    save_att.wait()


def on_device(hidden_rows, query_weight, kv_weight, cached_pages, page_dest, rec_rows):
    half = np.arange(HD) % (HD // 2)
    frequency = np.asarray(ROPE_BASE ** (-(half * 2.0 / HD)), np.float32).reshape(1, HD)
    depth = query_weight.shape[0]
    dma = pltpu.SemaphoreType.DMA
    hbm = pl.BlockSpec(memory_space=pltpu.HBM)
    attended, blended = pl.pallas_call(
        kernel,
        out_shape=(
            jax.ShapeDtypeStruct((REC, 2 * HD), BF16),
            jax.ShapeDtypeStruct((ROWS, 2 * HD), BF16),
        ),
        in_specs=[hbm] * 7,
        out_specs=(hbm, hbm),
        scratch_shapes=[
            pltpu.SMEM((1, SLOTS), jnp.int32),
            pltpu.VMEM((2 * NY, REC), jnp.int32),
            pltpu.VMEM((1, HD), F32),
            pltpu.VMEM((2 * DEPTH, 2 * HD), BF16),
            pltpu.VMEM((SLOTS * PAGE, 2 * HD), BF16),
            pltpu.VMEM((NX, REC, 2 * DEPTH), BF16),
            pltpu.VMEM((NY, 2, DEPTH // 2, 2 * HD), BF16),
            pltpu.VMEM((NX, ROWS, 2 * HD), BF16),
            pltpu.VMEM((NX - 1, ROWS, 2 * HD), BF16),
            pltpu.VMEM((2 * NY, ROWS, 2 * HD), BF16),
            pltpu.VMEM((HD, 2 * NY * ROWS), BF16),
            pltpu.VMEM((NX, 2 * REC, HD), BF16),
            pltpu.VMEM((NY, 2 * ROWS, 2 * REC), F32),
            pltpu.VMEM((NX, HD, 2 * REC), BF16),
            pltpu.VMEM((NX, 8, 2 * REC), F32),
            pltpu.VMEM((NX, HD, 2 * REC), BF16),
            pltpu.VMEM((NX, 8, 2 * REC), F32),
            pltpu.VMEM((REC, 2 * HD), BF16),
            dma((7,)),
            dma((2, 6)), dma((2, 6)),
            dma((2, 4, 2)), dma((2, 4, 2)),
            dma((8,)), dma((8,)),
            dma((3,)), dma((3,)),
            dma((8,)), dma((8,)),
            dma((8,)), dma((8,)),
            dma((NX,)), dma((NX,)),
            dma((NX,)), dma((NX,)),
            dma((NX,)), dma((NX,)),
        ],
        compiler_params=pltpu.CompilerParams(
            collective_id=0, has_side_effects=True, vmem_limit_bytes=64 * 1024 * 1024
        ),
    )(
        hidden_rows.reshape(REC, -1),
        query_weight.reshape(depth, 2 * HD),
        kv_weight,
        cached_pages.reshape(SLOTS * PAGE, 2 * HD),
        page_dest,
        rec_rows,
        jnp.asarray(frequency),
    )
    return attended.reshape(1, REC, 1, 2 * HD), blended.reshape(1, ROWS, 2 * HD)


def solution(mesh):
    placed = (
        P("seq", None, "store"),
        P("seq", "tp", "store"),
        P("store", "tp"),
        P("seq", "store", None, "tp"),
        P("seq", "store"),
        P(),
    )
    return jax.shard_map(
        on_device,
        mesh=mesh,
        in_specs=placed,
        out_specs=(P("seq", None, "tp", "store"), P("seq", "store", "tp")),
        check_vma=False,
    )
```

time: 260 us -> 58.8 us (0.23)
  the two profiles are of different devices: /device:TPU:1 before, /device:TPU:185 now
where the time goes in v1:
time: 58.8 us; the launch traced here: 58.6 us
  Pallas kernels  55.8 us (95%)
  local copies, waits for them, and re-layouts  2.14 us (4%)
  between operations  0.65 us (1%)
    pallas_call x1, Pallas kernels, on_device(): pl.pallas_call(kernel, out_shape=(jax.ShapeDtypeStruct((REC, 2 * HD), BF1...  55.8 us
    unnamed x4, local copies, waits for them, and re-layouts  2.14 us

profile of v1, /device:TPU:185, one launch (start us, length us, event | category | flops | bytes accessed | tf_op | source)
XLA Modules:
  0.0 58.6 jit_solution(16253179949717573259)
XLA Ops:
  0.6 55.8 %shard_map.86 = (bf16[128,256]{1,0:T(8,128)(2,1)}, bf16[128,256]{1,0:T(8,128)(2,1)}) custom-call(bf16[128,2048]{1,0:T(8,128)(2,1)} %bitcast.5, bf16[512,256]{1,0:T(8,128)(2,1)} %bitcast.6, bf16[2048,256]{1,0:T(8,128)(2,1)} %kvw_hbm.1, bf16[256,256]{1,0:T(8,128)(2,1)} %bitcast.7, s32[1,16]{1,0:T(1,128)} %dest_hbm.1, s32[16,128]{1,0:T(8,128)} %rec_hbm.1, ...), custom_call_target="tpu_custom_call" | custom-call | tf_op jit(solution)/shard_map/pallas_call | solution.py:432
  56.5 0.0 copy-start
  56.5 1.5 %copy.11 = bf16[1,128,1,256]{3,1,2,0:T(8,128)(2,1)} copy(bf16[1,128,1,256]{3,1,2,0:T(8,128)(2,1)} %bitcast.9) | data formatting | bytes 131072
  58.0 0.0 copy-done
  58.0 0.6 %copy.12 = bf16[1,128,256]{2,1,0:T(8,128)(2,1)} copy(bf16[1,128,256]{2,1,0:T(8,128)(2,1)S(1)} %bitcast.8) | data formatting | bytes 131072
Async XLA Ops:
  56.5 1.5 %copy-start = (bf16[128,256]{1,0:T(8,128)(2,1)S(1)}, bf16[128,256]{1,0:T(8,128)(2,1)}, u32[]{:S(2)}) copy-start(bf16[128,256]{1,0:T(8,128)(2,1)} %get-tuple-element.5) | copy-start | bytes 196612

commit v2 on v1

--- a/solution.py
+++ b/solution.py
@@ -36,7 +36,7 @@
     hid_hbm, wq_hbm, kvw_hbm, pages_hbm, dest_hbm, rec_hbm, freq_hbm,
     att_hbm, blend_hbm,
     dest_smem, rec_ref, freq_ref, kvw, pages, hall, wall, cont, cont_in, kv_all, v_t,
-    q_all, scores, o_out, s_out, o_in, s_in, att,
+    q_all, scores, probs, o_out, s_out, o_in, s_in, att,
     local_sem, h_send, h_recv, w_send, w_recv, ws_send, ws_recv,
     c_send, c_recv, kv_send, kv_recv, ks_send, ks_recv,
     q_send, q_recv, o_send, o_recv, s_send, s_recv,
@@ -98,6 +98,77 @@
     for off in (1, NY - 1):
         greet(dev(y_to=wrap(y + off, NY)))
     greet(dev(c_to=1 - c))
+
+    pl.semaphore_wait(barrier, 6)
+
+    right, left, far = wrap(x + 1, NX), wrap(x + NX - 1, NX), wrap(x + 2, NX)
+    other = 1 - c
+    up, down = dev(y_to=wrap(y + 1, NY)), dev(y_to=wrap(y + NY - 1, NY))
+
+    def half(at):
+        return pl.ds(at * DEPTH // 4, DEPTH // 4)
+
+    def weight_below(step):
+        return wall.at[wrap(y + NY - step, NY), c]
+
+    def weight_above(step):
+        return wall.at[wrap(y + step, NY), c]
+
+    def weight_up(src, block, step, at):
+        start(
+            remote(
+                src.at[half(at)], block.at[half(at)], w_send.at[0, step, at],
+                w_recv.at[0, step, at], up,
+            )
+        )
+
+    def weight_down(src, block, step, at):
+        start(
+            remote(
+                src.at[half(at)], block.at[half(at)], w_send.at[1, step, at],
+                w_recv.at[1, step, at], down,
+            )
+        )
+
+    def weight_core(src, block, step):
+        start(remote(src, block, ws_send.at[step], ws_recv.at[step], dev(c_to=other)))
+
+    own = wall.at[y, c]
+    weight_up(wq_hbm, own, 0, 0)
+    weight_down(wq_hbm, own, 0, 1)
+    weight_up(wq_hbm, own, 0, 1)
+    weight_down(wq_hbm, own, 0, 0)
+    weight_core(wq_hbm, own, 0)
+
+    def weight_relay(step, at):
+        arrived(weight_below(step).at[half(at)], w_recv.at[0, step - 1, at])
+        if step < 3 or at == 0:
+            weight_up(weight_below(step), weight_below(step), step, at)
+        arrived(weight_above(step).at[half(1 - at)], w_recv.at[1, step - 1, 1 - at])
+        if step < 3 or at == 0:
+            weight_down(weight_above(step), weight_above(step), step, 1 - at)
+        if at == 1:
+            weight_core(weight_below(step), weight_below(step), 2 * step - 1)
+            weight_core(weight_above(step), weight_above(step), 2 * step)
+
+    def piece(at):
+        return pl.ds(at * DEPTH // 2, DEPTH // 2)
+
+    def hidden_right(src, block, step, at):
+        start(
+            remote(
+                src.at[:, piece(at)], block.at[:, piece(at)], h_send.at[0, step],
+                h_recv.at[0, step], dev(x_to=right),
+            )
+        )
+
+    def hidden_left(src, block, step, at):
+        start(
+            remote(
+                src.at[:, piece(at)], block.at[:, piece(at)], h_send.at[1, step],
+                h_recv.at[1, step], dev(x_to=left),
+            )
+        )
 
     load_rec.wait()
     load_freq.wait()
@@ -140,89 +211,21 @@
         term = term + jnp.dot(pick_page.astype(BF16), pages[...], preferred_element_type=F32)
         cont[part] = term.astype(BF16)
 
-    pl.semaphore_wait(barrier, 6)
-
     for off in range(1, NX):
         x_to = wrap(x + off, NX)
         start(
             remote(
                 cont.at[x_to], cont_in.at[off - 1], c_send.at[off - 1], c_recv.at[off - 1],
                 dev(x_to=x_to),
-            )
-        )
-
-    right, left, far = wrap(x + 1, NX), wrap(x + NX - 1, NX), wrap(x + 2, NX)
-    other = 1 - c
-    up, down = dev(y_to=wrap(y + 1, NY)), dev(y_to=wrap(y + NY - 1, NY))
-
-    def half(at):
-        return pl.ds(at * DEPTH // 4, DEPTH // 4)
-
-    def weight_below(step):
-        return wall.at[wrap(y + NY - step, NY), c]
-
-    def weight_above(step):
-        return wall.at[wrap(y + step, NY), c]
-
-    def weight_up(src, block, step, at):
-        start(
-            remote(
-                src.at[half(at)], block.at[half(at)], w_send.at[0, step, at],
-                w_recv.at[0, step, at], up,
-            )
-        )
-
-    def weight_down(src, block, step, at):
-        start(
-            remote(
-                src.at[half(at)], block.at[half(at)], w_send.at[1, step, at],
-                w_recv.at[1, step, at], down,
-            )
-        )
-
-    def weight_core(src, block, step):
-        start(remote(src, block, ws_send.at[step], ws_recv.at[step], dev(c_to=other)))
-
-    own = wall.at[y, c]
-    weight_up(wq_hbm, own, 0, 0)
-    weight_down(wq_hbm, own, 0, 1)
-    weight_up(wq_hbm, own, 0, 1)
-    weight_down(wq_hbm, own, 0, 0)
-    weight_core(wq_hbm, own, 0)
-
-    def weight_relay(step):
-        for at in range(2):
-            arrived(weight_below(step).at[half(at)], w_recv.at[0, step - 1, at])
-            if step < 3 or at == 0:
-                weight_up(weight_below(step), weight_below(step), step, at)
-            arrived(weight_above(step).at[half(1 - at)], w_recv.at[1, step - 1, 1 - at])
-            if step < 3 or at == 0:
-                weight_down(weight_above(step), weight_above(step), step, 1 - at)
-        weight_core(weight_below(step), weight_below(step), 2 * step - 1)
-        weight_core(weight_above(step), weight_above(step), 2 * step)
-
-    def piece(at):
-        return pl.ds(at * DEPTH // 2, DEPTH // 2)
-
-    def hidden_right(src, block, step, at):
-        start(
-            remote(
-                src.at[:, piece(at)], block.at[:, piece(at)], h_send.at[0, step],
-                h_recv.at[0, step], dev(x_to=right),
-            )
-        )
-
-    def hidden_left(src, block, step, at):
-        start(
-            remote(
-                src.at[:, piece(at)], block.at[:, piece(at)], h_send.at[1, step],
-                h_recv.at[1, step], dev(x_to=left),
             )
         )
 
     for at in range(4):
         hidden_right(hid_hbm, hall.at[x], at, at)
         hidden_left(hid_hbm, hall.at[x], 3 - at, 3 - at)
+
+    weight_relay(1, 0)
+    weight_relay(1, 1)
 
     total = cont[x].astype(F32)
     for off in range(1, NX):
@@ -267,18 +270,20 @@
     pass_down(kv_all.at[sq], 0)
     pass_core(kv_all.at[sq], 0)
 
-    weight_relay(1)
-    for at in range(2):
+    def hidden_relay(at):
         arrived(hall.at[left, :, piece(at)], h_recv.at[0, at])
         hidden_right(hall.at[left], hall.at[left], 4 + at, at)
         arrived(hall.at[right, :, piece(3 - at)], h_recv.at[1, 3 - at])
         hidden_left(hall.at[right], hall.at[right], 5 - at, 3 - at)
 
-    weight_relay(2)
+    weight_relay(2, 0)
+    hidden_relay(0)
+    weight_relay(2, 1)
     relay(1)
-    weight_relay(3)
+    hidden_relay(1)
+    weight_relay(3, 0)
     relay(2)
-    relay(3)
+    weight_relay(3, 1)
 
     for at in range(2):
         arrived(hall.at[left, :, piece(2 + at)], h_recv.at[0, 2 + at])
@@ -304,6 +309,7 @@
         arrived(wall.at[above_at, other], ws_recv.at[2 * step])
         q_sum = q_sum + term(above_at)
     opposite = wrap(y + 4, NY)
+    relay(3)
     arrived(weight_below(4).at[half(0)], w_recv.at[0, 3, 0])
     arrived(weight_below(4).at[half(1)], w_recv.at[1, 3, 1])
     weight_core(weight_below(4), weight_below(4), 7)
@@ -339,9 +345,7 @@
 
     pair = 2 * ROWS
     key_row = lax.broadcasted_iota(jnp.int32, (pair, 2 * REC), 0)
-    key_place = (
-        (2 * y + key_row // ROWS) * PASSAGE + x * ROWS + wrap(key_row, ROWS)
-    )
+    key_place = key_row // ROWS * PASSAGE + x * ROWS + wrap(key_row, ROWS)
     query_place = jnp.concatenate([chosen, chosen], axis=1) + sq * PASSAGE
 
     def attend(off):
@@ -350,38 +354,23 @@
             arrived(q_all.at[to], q_recv.at[NX - off])
         query = q_all[to]
 
-        def score(at):
-            keys = kv_all[pl.ds(2 * at, 2), :, :HD].reshape(pair, HD)
-            return lax.dot_general(
+        top = jnp.full((8, 2 * REC), MASKED, F32)
+        for at in range(NY):
+            keys = kv_all[2 * at : 2 * at + 2, :, :HD].reshape(pair, HD)
+            value = lax.dot_general(
                 keys, query, (((1,), (1,)), ((), ())), preferred_element_type=F32
             )
-
-        def first(at, top):
-            value = score(at)
+            value = jnp.where(key_place + 2 * at * PASSAGE <= query_place, value, MASKED)
             scores[at] = value
-            return jnp.maximum(top, jnp.max(value.reshape(pair // 8, 8, 2 * REC), axis=0))
-
-        top = lax.fori_loop(0, y, first, jnp.full((8, 2 * REC), MASKED, F32))
-        value = jnp.where(key_place <= query_place, score(y), MASKED)
-        scores[y] = value
-        top = jnp.maximum(top, jnp.max(value.reshape(pair // 8, 8, 2 * REC), axis=0))
+            top = jnp.maximum(top, jnp.max(value.reshape(pair // 8, 8, 2 * REC), axis=0))
         top = jnp.max(top, axis=0, keepdims=True)
-
-        def second(at, carry):
-            sums, mixture = carry
+        sums = jnp.zeros((8, 2 * REC), F32)
+        for at in range(NY):
             weights = jnp.exp2(scores[at] - top)
             sums = sums + jnp.sum(weights.reshape(pair // 8, 8, 2 * REC), axis=0)
-            values = v_t[:, pl.ds(pl.multiple_of(at * pair, pair), pair)]
-            mixture = mixture + jnp.dot(
-                values, weights.astype(BF16), preferred_element_type=F32
-            )
-            return sums, mixture
-
-        sums, mixture = lax.fori_loop(
-            0, y + 1, second,
-            (jnp.zeros((8, 2 * REC), F32), jnp.zeros((HD, 2 * REC), F32)),
-        )
+            probs[at * pair : (at + 1) * pair] = weights.astype(BF16)
         sums = jnp.sum(sums, axis=0, keepdims=True)
+        mixture = jnp.dot(v_t[...], probs[...], preferred_element_type=F32)
         o_out[off] = mixture.astype(BF16)
         s_out[off, 0:1, :] = top
         s_out[off, 1:2, :] = sums
@@ -395,9 +384,9 @@
             )
 
     attend(0)
+    attend(2)
     attend(1)
     attend(3)
-    attend(2)
 
     for off in (1, 3, 2):
         arrived(o_in.at[off], o_recv.at[off])
@@ -451,6 +440,7 @@
             pltpu.VMEM((HD, 2 * NY * ROWS), BF16),
             pltpu.VMEM((NX, 2 * REC, HD), BF16),
             pltpu.VMEM((NY, 2 * ROWS, 2 * REC), F32),
+            pltpu.VMEM((2 * NY * ROWS, 2 * REC), BF16),
             pltpu.VMEM((NX, HD, 2 * REC), BF16),
             pltpu.VMEM((NX, 8, 2 * REC), F32),
             pltpu.VMEM((NX, HD, 2 * REC), BF16),

time: 58.8 us -> 52.8 us (0.90)
  the two profiles are of different devices: /device:TPU:185 before, /device:TPU:1 now
where the time goes in v2:
time: 52.8 us; the launch traced here: 52.6 us
  Pallas kernels  49.8 us (94%)
  local copies, waits for them, and re-layouts  2.14 us (4%)
  between operations  0.65 us (1%)
    pallas_call x1, Pallas kernels, on_device(): pl.pallas_call(kernel, out_shape=(jax.ShapeDtypeStruct((REC, 2 * HD), BF1...  49.8 us
    unnamed x4, local copies, waits for them, and re-layouts  2.14 us

profile of v2, /device:TPU:1, one launch (start us, length us, event | category | flops | bytes accessed | tf_op | source)
XLA Modules:
  0.0 52.6 jit_solution(13535937706929479815)
XLA Ops:
  0.6 49.8 %shard_map.86 = (bf16[128,256]{1,0:T(8,128)(2,1)}, bf16[128,256]{1,0:T(8,128)(2,1)}) custom-call(bf16[128,2048]{1,0:T(8,128)(2,1)} %bitcast.5, bf16[512,256]{1,0:T(8,128)(2,1)} %bitcast.6, bf16[2048,256]{1,0:T(8,128)(2,1)} %kvw_hbm.1, bf16[256,256]{1,0:T(8,128)(2,1)} %bitcast.7, s32[1,16]{1,0:T(1,128)} %dest_hbm.1, s32[16,128]{1,0:T(8,128)} %rec_hbm.1, ...), custom_call_target="tpu_custom_call" | custom-call | tf_op jit(solution)/shard_map/pallas_call | solution.py:421
  50.5 0.0 copy-start
  50.5 1.5 %copy.11 = bf16[1,128,1,256]{3,1,2,0:T(8,128)(2,1)} copy(bf16[1,128,1,256]{3,1,2,0:T(8,128)(2,1)} %bitcast.9) | data formatting | bytes 131072
  52.0 0.0 copy-done
  52.0 0.6 %copy.12 = bf16[1,128,256]{2,1,0:T(8,128)(2,1)} copy(bf16[1,128,256]{2,1,0:T(8,128)(2,1)S(1)} %bitcast.8) | data formatting | bytes 131072
Async XLA Ops:
  50.5 1.5 %copy-start = (bf16[128,256]{1,0:T(8,128)(2,1)S(1)}, bf16[128,256]{1,0:T(8,128)(2,1)}, u32[]{:S(2)}) copy-start(bf16[128,256]{1,0:T(8,128)(2,1)} %get-tuple-element.5) | copy-start | bytes 196612
